TPU v7x, 128 devices: a whole 4x4x4 slice. The times are simulated.
128 devices in a mesh: wide: 64 (over z, y, x), narrow: 2 (over core).
Axes of the slice: x: 4, y: 4, z: 4, core: 2. Of those that a mesh axis runs over, the one named last changes fastest.
Arguments:
- voltages: bfloat16 [1024, 2, 2, 779, 192], P(('narrow', 'wide')), may hold values from -8 to 8
- flags: int32 [512], replicated, may hold values 0 or 1
- tiles: int32 [10, 2], P('narrow'), may hold values from 0 to 3, as said below
Outputs:
- visibilities: float32 [10, 384, 2, 65536], P('narrow', 'wide')
Inputs may be any that keep to these rules, and one draw needn't show every extreme that they name: `tiles`: every pair (r, c) with r >= c of the 4 groups stands exactly once in the whole list.
All inputs are finite; a program needn't handle non-finite values.
Results may differ from a plain program's by a relative error of at most 0.0006.
Values may be sent and summed in bfloat16 or wider, within the bound.
No kernel may reach another device: no remote copies, remote signals or barrier semaphores. Data moves between devices by JAX's collectives and lax.ppermute only.
A program may use at most 192 MiB of HBM per device.

v0:
```python
import functools

import jax
import jax.numpy as jnp
import numpy as np
from jax import lax
from jax.experimental import pallas as pl
from jax.experimental.pallas import tpu as pltpu
from jax.sharding import PartitionSpec as P

F = 192
TAPS = 12
COARSE = 2
HEAD = 256
WIDE = 64
LOCAL = 8
PER = 6
LANES = 128
MADE = 15
TOGETHER = 4
SPLIT = (4, 2)
VMEM_BYTES = 60 * 2**20


def prototype():
    length = TAPS * F
    sample = np.arange(length, dtype=np.float64)
    centre = (length - 1) / 2.0
    taper = np.sinc((sample - centre) / F)
    window = 0.5 - 0.5 * np.cos(2.0 * np.pi * (sample + 0.5) / length)
    shaped = taper * window
    shaped = shaped * np.sqrt(F / np.sum(shaped * shaped))
    return shaped.reshape(TAPS, F)


def filter_table():
    taps = prototype().astype(np.float32)
    both = np.concatenate([taps, taps], axis=1)
    return np.ascontiguousarray(np.broadcast_to(both[:, None, :], (TAPS, 8, 2 * F)))


def transform_table():
    k = np.arange(F)
    angle = 2.0 * np.pi * ((k[:, None] * k[None, :]) % F) / F
    cosine, sine = np.cos(angle), np.sin(angle)
    real = np.concatenate([cosine, sine], axis=1)
    imag = np.concatenate([-sine, cosine], axis=1)
    rows = np.stack([real, imag], axis=1).reshape(2 * F, 2 * F) / np.sqrt(float(F))
    rows = rows.astype(np.float32)
    high = rows.astype(jnp.bfloat16)
    low = (rows - high.astype(np.float32)).astype(jnp.bfloat16)
    return np.concatenate([high, high, low], axis=1)


def spectra_kernel(first, count, split, flags_ref, volt_ref, taps_ref, table_ref, *rest):
    parts = len(split)
    outs, results = rest[:parts], rest[parts : 2 * parts]
    scratch = rest[2 * parts :]
    series, framed = scratch[:TOGETHER], scratch[TOGETHER : 2 * TOGETHER]
    volts, turned, in_sem, out_sem = scratch[2 * TOGETHER :]
    device = lax.axis_index("narrow") * WIDE + lax.axis_index("wide")
    slots = volts.shape[0]
    width = count + LANES
    total = COARSE * LOCAL
    span = volts.shape[-1]

    def incoming(n):
        slot = lax.rem(n, slots)
        source = volt_ref.at[lax.rem(n, LOCAL), n // LOCAL]
        if span < volt_ref.shape[-1]:
            source = source.at[:, :, pl.ds(0, span)]
        return pltpu.make_async_copy(source, volts.at[slot], in_sem.at[slot])

    def outgoing(c):
        half = WIDE // COARSE
        return [
            pltpu.make_async_copy(held.at[c], out.at[pl.ds(c * half, half)], out_sem.at[c, which])
            for which, (held, out) in enumerate(zip(results, outs))
        ]

    def transform(slot, i, series, framed):
        keep = (1 - flags_ref[(device * LOCAL + i) // 2]).astype(jnp.float32)
        for tile in range(width // LANES):
            start = first + tile * LANES
            stop = min(start + LANES, span)
            pieces = [volts[slot, p, :, start:stop].astype(jnp.float32) for p in range(2)]
            rows = jnp.concatenate(pieces, axis=0)
            for column in range(3):
                series[column, tile * LANES : tile * LANES + stop - start, :] = rows[
                    column * LANES : (column + 1) * LANES
                ].T
        for column in range(3):
            lanes = slice(column * LANES, (column + 1) * LANES)
            taps = [taps_ref[m, :, lanes] for m in range(TAPS)]
            for start in range(0, count, 64):
                value = None
                for m in range(TAPS):
                    tap = jnp.concatenate([taps[m]] * 8, axis=0)
                    term = tap * series[column, start + m : start + m + 64, :]
                    value = term if value is None else value + term
                top = value.astype(jnp.bfloat16)
                rest_part = (value - top.astype(jnp.float32)).astype(jnp.bfloat16)
                for third, half in enumerate((top, rest_part, top)):
                    at = third * 2 * F + column * LANES
                    framed[start : start + 64, at : at + LANES] = half
        product = lax.dot_general(
            table_ref[...], framed[...], (((1,), (1,)), ((), ())), preferred_element_type=jnp.float32
        )
        product = product * keep
        for tile in range(count // LANES):
            turned[tile, pl.ds(i, 2 * F, stride=LOCAL), :] = product[
                :, tile * LANES : (tile + 1) * LANES
            ]

    def step(q, carry):
        n = q * TOGETHER
        c = n // LOCAL

        @pl.when(n + TOGETHER < total)
        def _():
            for k in range(TOGETHER):
                incoming(n + TOGETHER + k).start()

        for k in range(TOGETHER):
            incoming(n + k).wait()
        for k in range(TOGETHER):
            transform(lax.rem(n + k, slots), lax.rem(n, LOCAL) + k, series[k], framed[k])

        @pl.when(lax.rem(n, LOCAL) == LOCAL - TOGETHER)
        def _():
            for tile in range(count // LANES):
                value = turned[tile].astype(jnp.bfloat16)
                value = value.reshape(WIDE // COARSE, PER * 2 * LOCAL, LANES)
                lanes = slice(tile * LANES, (tile + 1) * LANES)
                at = 0
                for held, channels in zip(results, split):
                    rows = channels * 2 * LOCAL
                    held[c, :, :, lanes] = value[:, at : at + rows, :]
                    at += rows
            for copy in outgoing(c):
                copy.start()

        return carry

    for k in range(TOGETHER):
        incoming(k).start()
    lax.fori_loop(0, total // TOGETHER, step, 0)
    for c in range(COARSE):
        for copy in outgoing(c):
            copy.wait()


def spectra(flags, voltages, taps, table, first, count, split):
    half = WIDE // COARSE
    reach = first + count + TAPS - 1
    span = min(-(-reach // LANES) * LANES, voltages.shape[-1])
    sizes = [(channels * 2 * LOCAL, count) for channels in split]
    smem, vmem, hbm = (
        pl.BlockSpec(memory_space=m) for m in (pltpu.SMEM, pltpu.VMEM, pl.ANY)
    )
    return pl.pallas_call(
        functools.partial(spectra_kernel, first, count, split),
        out_shape=[jax.ShapeDtypeStruct((WIDE,) + size, jnp.bfloat16) for size in sizes],
        in_specs=[smem, hbm, vmem, vmem],
        out_specs=[hbm] * len(split),
        scratch_shapes=[pltpu.VMEM((COARSE, half) + size, jnp.bfloat16) for size in sizes]
        + [pltpu.VMEM((3, count + LANES, LANES), jnp.float32)] * TOGETHER
        + [pltpu.VMEM((count, 6 * F), jnp.bfloat16)] * TOGETHER
        + [
            pltpu.VMEM((2 * TOGETHER, 2, F, span), jnp.bfloat16),
            pltpu.VMEM((count // LANES, 2 * F * LOCAL, LANES), jnp.float32),
            pltpu.SemaphoreType.DMA((2 * TOGETHER,)),
            pltpu.SemaphoreType.DMA((COARSE, len(split))),
        ],
        compiler_params=pltpu.CompilerParams(vmem_limit_bytes=VMEM_BYTES),
        cost_estimate=pl.CostEstimate(
            flops=16 * 2 * 3 * F * F * 4 * count, bytes_accessed=32 * F * count * 4, transcendentals=0
        ),
        name="spectra",
    )(flags, voltages, taps, table)


def correlate_kernel(scale, base, tiles_ref, own1, own2, other1, other2, *rest):
    out_hbm, heads, tails, groups, made, in_sem, out_sem = rest[-7:]
    mine = lax.axis_index("narrow")
    channels = heads.shape[0]
    count = out_hbm.shape[0]
    slots = made.shape[0]
    head = heads.shape[-1]

    def incoming(j):
        head_rows = pl.ds(16 * (base + j), 16)
        rows = pl.ds(16 * j, 16)
        copies = []
        for side, (first, second) in enumerate(((own1, own2), (other1, other2))):
            copies.append(
                pltpu.make_async_copy(first.at[:, head_rows, :], heads.at[j, side], in_sem.at[j, side, 0])
            )
            copies.append(
                pltpu.make_async_copy(second.at[:, rows, :], tails.at[j, side], in_sem.at[j, side, 1])
            )
        return copies

    def outgoing(j, t):
        slot = (j * count + t) % slots
        return pltpu.make_async_copy(
            made.at[slot], out_hbm.at[t, base + j], out_sem.at[slot]
        )

    for copy in incoming(0):
        copy.start()
    dims = (((1,), (1,)), ((), ()))
    for j in range(channels):
        for copy in incoming(j):
            copy.wait()
        if j + 1 < channels:
            for copy in incoming(j + 1):
                copy.start()
        hold = j % 2
        for side in range(2):
            half = mine if side == 0 else 1 - mine
            for part in range(2):
                sources = slice(part * 32, part * 32 + 32)
                for at, held in ((0, heads), (head, tails)):
                    value = held[j, side, sources].astype(jnp.float32)
                    size = value.shape[2]
                    for which in range(2):
                        piece = value[:, which * 8 : which * 8 + 8, :].reshape(256, size)
                        groups[hold, half * 2 + part, which * 256 : which * 256 + 256, at : at + size] = (
                            piece.astype(jnp.bfloat16)
                        )
        for t in range(count):
            n = j * count + t
            slot = n % slots
            rows = groups[hold, tiles_ref[0, t]]
            column = tiles_ref[1, t]
            with_real = lax.dot_general(
                rows, groups[hold, column, 0:256, :], dims, preferred_element_type=jnp.float32
            )
            with_imag = lax.dot_general(
                rows, groups[hold, column, 256:512, :], dims, preferred_element_type=jnp.float32
            )
            real = (with_real[0:256] + with_imag[256:512]) * scale
            imag = (with_real[256:512] - with_imag[0:256]) * scale
            if n >= slots:
                outgoing((n - slots) // count, (n - slots) % count).wait()
            for side in range(2):
                lanes = slice(side * LANES, side * LANES + LANES)
                made[slot, pl.ds(2 * side, 256, stride=4), :] = real[:, lanes]
                made[slot, pl.ds(2 * side + 1, 256, stride=4), :] = imag[:, lanes]
            outgoing(j, t).start()
    for n in range(max(channels * count - slots, 0), channels * count):
        outgoing(n // count, n % count).wait()


def correlate(tiles, own1, own2, other1, other2, base, before):
    head, tail = own1.shape[-1], own2.shape[-1]
    spectra_count = head + tail
    count = tiles.shape[1]
    smem, hbm = (pl.BlockSpec(memory_space=m) for m in (pltpu.SMEM, pl.ANY))
    operands = [tiles, own1, own2, other1, other2]
    aliases = {}
    if before is not None:
        operands.append(before)
        aliases = {5: 0}
    channels = own2.shape[1] // 16
    return pl.pallas_call(
        functools.partial(correlate_kernel, 1.0 / spectra_count, base),
        out_shape=jax.ShapeDtypeStruct((count, PER, 1024, LANES), jnp.float32),
        in_specs=[smem] + [hbm] * (len(operands) - 1),
        out_specs=hbm,
        scratch_shapes=[
            pltpu.VMEM((channels, 2, WIDE, 16, head), jnp.bfloat16),
            pltpu.VMEM((channels, 2, WIDE, 16, tail), jnp.bfloat16),
            pltpu.VMEM((2, 4, 512, spectra_count), jnp.bfloat16),
            pltpu.VMEM((MADE, 1024, LANES), jnp.float32),
            pltpu.SemaphoreType.DMA((channels, 2, 2)),
            pltpu.SemaphoreType.DMA((MADE,)),
        ],
        input_output_aliases=aliases,
        compiler_params=pltpu.CompilerParams(vmem_limit_bytes=VMEM_BYTES),
        cost_estimate=pl.CostEstimate(
            flops=5 * channels * 8 * 256 * 256 * spectra_count, bytes_accessed=20 * 2**20, transcendentals=0
        ),
        name="correlate",
    )(*operands)


def body(voltages, flags, tiles):
    spectra_count = voltages.shape[3] - TAPS + 1
    count = tiles.shape[0]
    taps = jnp.asarray(filter_table())
    table = jnp.asarray(transform_table())
    by_time = jnp.transpose(voltages, (0, 1, 2, 4, 3))
    pairs = jnp.transpose(tiles)

    def exchange(value):
        return lax.all_to_all(value, "wide", split_axis=0, concat_axis=0, tiled=True)

    def swap(value):
        return lax.ppermute(value, "narrow", [(0, 1), (1, 0)])

    (head,) = spectra(flags, by_time, taps, table, 0, HEAD, (PER,))
    head, by_time = lax.optimization_barrier((head, by_time))
    own_head = exchange(head)
    tails = spectra(flags, by_time, taps, table, HEAD, spectra_count - HEAD, SPLIT)
    own_head, first, second = lax.optimization_barrier((own_head, *tails))
    own_first = exchange(first)
    other_head = swap(own_head)
    own_first, second = lax.optimization_barrier((own_first, second))
    own_second = exchange(second)
    other_first = swap(own_first)
    out = correlate(pairs, own_head, own_first, other_head, other_first, 0, None)
    own_second, out = lax.optimization_barrier((own_second, out))
    other_second = swap(own_second)
    out = correlate(pairs, own_head, own_second, other_head, other_second, SPLIT[0], out)
    out = out.reshape(count, PER, 512, 2, LANES)
    out = jnp.transpose(out, (0, 1, 3, 2, 4))
    return out.reshape(count, PER, 2, 512 * LANES)


def solution(mesh):
    return jax.shard_map(
        body,
        mesh=mesh,
        in_specs=(P(("narrow", "wide"), None, None, None, None), P(), P("narrow", None)),
        out_specs=P("narrow", "wide", None, None),
        check_vma=False,
    )
```

profile of v0, /device:TPU:1, one launch (start us, length us, event | category | flops | bytes accessed | tf_op | source)
XLA Modules:
  0.0 182.8 jit_solution(17941850413479817993)
XLA Ops:
  0.0 16.8 %spectra.2 = bf16[64,96,256]{2,1,0:T(8,128)(2,1)} custom-call(s32[512]{0:T(512)} %flags_ref.3, bf16[8,2,2,192,779]{4,3,2,1,0:T(8,128)(2,1)} %bitcast.7, f32[12,8,384]{2,1,0:T(8,128)} %constant.4.clone.taps_ref, bf16[384,1152]{1,0:T(8,128)(2,1)} %constant.5.clone.table_ref), custom_call_target="tpu_custom_call" | custom-call | flops 3623878656 | bytes 6291456 | tf_op jit(solution)/shard_map/spectra/pallas_call | solution.py:161
  16.8 12.0 %all-to-all-start = ((bf16[64,96,256]{2,1,0:T(8,128)(2,1)}), bf16[64,96,256]{2,1,0:T(8,128)(2,1)S(1)}, u32[]{:S(2)}, u32[]{:S(2)}) async-start(bf16[64,96,256]{2,1,0:T(8,128)(2,1)} %spectra.2), calls=%async_computation | async-start | bytes 6291456 | tf_op jit(solution)/shard_map/all_to_all | solution.py:298
  28.8 29.3 %spectra.3 = (bf16[64,64,512]{2,1,0:T(8,128)(2,1)}, bf16[64,32,512]{2,1,0:T(8,128)(2,1)}) custom-call(s32[512]{0:T(512)} %flags_ref.3, bf16[8,2,2,192,779]{4,3,2,1,0:T(8,128)(2,1)} %bitcast.8, f32[12,8,384]{2,1,0:T(8,128)} %constant.4.clone.taps_ref, bf16[384,1152]{1,0:T(8,128)(2,1)} %constant.5.clone.table_ref), custom_call_target="tpu_custom_call" | custom-call | flops 7247757312 | bytes 12582912 | tf_op jit(solution)/shard_map/spectra/pallas_call | solution.py:161
  58.1 10.1 %all-to-all-done.own1 = bf16[64,96,256]{2,1,0:T(8,128)(2,1)S(1)} async-done(((bf16[64,96,256]{2,1,0:T(8,128)(2,1)}), bf16[64,96,256]{2,1,0:T(8,128)(2,1)S(1)}, u32[]{:S(2)}, u32[]{:S(2)}) %all-to-all-start) | async-done | bytes 3145760 | tf_op jit(solution)/shard_map/all_to_all | solution.py:298
  68.2 0.0 copy-start
  68.2 60.4 %all_to_all.15.own2 = bf16[64,64,512]{2,1,0:T(8,128)(2,1)} all-to-all(bf16[64,64,512]{2,1,0:T(8,128)(2,1)} %get-tuple-element.21), channel_id=1, replica_groups=mesh['wide'=64,'narrow'=2] {'wide'}, dimensions={0} | all-to-all | bytes 8388608 | tf_op jit(solution)/shard_map/all_to_all | solution.py:298
  128.6 2.3 %collective-permute-start.1 = (bf16[64,64,512]{2,1,0:T(8,128)(2,1)}, bf16[64,64,512]{2,1,0:T(8,128)(2,1)}, u32[]{:S(2)}, u32[]{:S(2)}) collective-permute-start(bf16[64,64,512]{2,1,0:T(8,128)(2,1)} %all_to_all.15.own2), channel_id=1, source_target_pairs={{0,1},{1,0},{2,3},{3,2},{4,5},{5,4},{6,7},{7,6},{8,9},{9,8},{10,11... | collective-permute-start | bytes 12582920 | tf_op jit(solution)/shard_map/ppermute | solution.py:301
  131.0 0.0 copy-done
  131.0 0.0 collective-permute-start
  131.0 6.0 %all-to-all-start.2 = ((bf16[64,32,512]{2,1,0:T(8,128)(2,1)}), bf16[64,32,512]{2,1,0:T(8,128)(2,1)}, u32[]{:S(2)}, u32[]{:S(2)}) async-start(bf16[64,32,512]{2,1,0:T(8,128)(2,1)} %get-tuple-element.23), calls=%async_computation.2 | async-start | bytes 4194304 | tf_op jit(solution)/shard_map/all_to_all | solution.py:298
  137.0 5.2 %collective-permute-done.other1 = bf16[64,96,256]{2,1,0:T(8,128)(2,1)} collective-permute-done((bf16[64,96,256]{2,1,0:T(8,128)(2,1)S(1)}, bf16[64,96,256]{2,1,0:T(8,128)(2,1)}, u32[]{:S(2)}, u32[]{:S(2)}) %collective-permute-start) | collective-permute-done | bytes 3145760 | tf_op jit(solution)/shard_map/ppermute | solution.py:301
  142.3 0.3 collective-permute-done.1.other2
  142.6 18.1 %correlate.2.rest_0_ = f32[5,6,1024,128]{3,2,1,0:T(8,128)} custom-call(s32[2,5]{1,0:T(2,128)} %bitcast.9, bf16[64,96,256]{2,1,0:T(8,128)(2,1)} %copy-done, bf16[64,64,512]{2,1,0:T(8,128)(2,1)} %all_to_all.15.own2, bf16[64,96,256]{2,1,0:T(8,128)(2,1)} %collective-permute-done.other1, bf16[64,64,512]{2,1,0:T(8,128)(2,1)} %collective-permute-done.1.other2), custom_call_target="tpu_custom_call" | custom-call | flops 8053063680 | bytes 20971520 | tf_op jit(solution)/shard_map/correlate/pallas_call | solution.py:267
  160.7 4.8 %all-to-all-done.2.own2 = bf16[64,32,512]{2,1,0:T(8,128)(2,1)} async-done(((bf16[64,32,512]{2,1,0:T(8,128)(2,1)}), bf16[64,32,512]{2,1,0:T(8,128)(2,1)}, u32[]{:S(2)}, u32[]{:S(2)}) %all-to-all-start.2) | async-done | bytes 2097184 | tf_op jit(solution)/shard_map/all_to_all | solution.py:298
  165.6 2.3 %collective-permute-start.2 = (bf16[64,32,512]{2,1,0:T(8,128)(2,1)}, bf16[64,32,512]{2,1,0:T(8,128)(2,1)S(1)}, u32[]{:S(2)}, u32[]{:S(2)}) collective-permute-start(bf16[64,32,512]{2,1,0:T(8,128)(2,1)} %all-to-all-done.2.own2), channel_id=1, source_target_pairs={{0,1},{1,0},{2,3},{3,2},{4,5},{5,4},{6,7},{7,6},{8,9},{9,8},{10,11... | collective-permute-start | bytes 6291464 | tf_op jit(solution)/shard_map/ppermute | solution.py:301
  167.9 4.0 %collective-permute-done.2.other2 = bf16[64,32,512]{2,1,0:T(8,128)(2,1)S(1)} collective-permute-done((bf16[64,32,512]{2,1,0:T(8,128)(2,1)}, bf16[64,32,512]{2,1,0:T(8,128)(2,1)S(1)}, u32[]{:S(2)}, u32[]{:S(2)}) %collective-permute-start.2) | collective-permute-done | bytes 2097184 | tf_op jit(solution)/shard_map/ppermute | solution.py:301
  171.9 0.0 copy-start.1
  171.9 1.3 copy-done.1
  173.2 9.5 %correlate.3 = f32[5,6,1024,128]{3,2,1,0:T(8,128)} custom-call(s32[2,5]{1,0:T(2,128)} %bitcast.10, bf16[64,96,256]{2,1,0:T(8,128)(2,1)} %copy-done, bf16[64,32,512]{2,1,0:T(8,128)(2,1)} %all-to-all-done.2.own2, bf16[64,96,256]{2,1,0:T(8,128)(2,1)} %collective-permute-done.other1, bf16[64,32,512]{2,1,0:T(8,128)(2,1)} %copy-done.1, ...), custom_call_target="tpu_custom_call", output_to_operand_aliasing={{}: (5, {})} | custom-call | flops 4026531840 | bytes 20971520 | tf_op jit(solution)/shard_map/correlate/pallas_call | solution.py:267
Async XLA Ops:
  16.8 51.4 %all-to-all-start = ((bf16[64,96,256]{2,1,0:T(8,128)(2,1)}), bf16[64,96,256]{2,1,0:T(8,128)(2,1)S(1)}, u32[]{:S(2)}, u32[]{:S(2)}) async-start(bf16[64,96,256]{2,1,0:T(8,128)(2,1)} %spectra.2), calls=%async_computation | async-start | bytes 6291456 | tf_op jit(solution)/shard_map/all_to_all | solution.py:298
  68.2 62.8 %copy-start = (bf16[64,96,256]{2,1,0:T(8,128)(2,1)}, bf16[64,96,256]{2,1,0:T(8,128)(2,1)S(1)}, u32[]{:S(2)}) copy-start(bf16[64,96,256]{2,1,0:T(8,128)(2,1)S(1)} %all-to-all-done.own1) | copy-start | bytes 9437188
  128.6 14.0 %collective-permute-start.1 = (bf16[64,64,512]{2,1,0:T(8,128)(2,1)}, bf16[64,64,512]{2,1,0:T(8,128)(2,1)}, u32[]{:S(2)}, u32[]{:S(2)}) collective-permute-start(bf16[64,64,512]{2,1,0:T(8,128)(2,1)} %all_to_all.15.own2), channel_id=1, source_target_pairs={{0,1},{1,0},{2,3},{3,2},{4,5},{5,4},{6,7},{7,6},{8,9},{9,8},{10,11... | collective-permute-start | bytes 12582920 | tf_op jit(solution)/shard_map/ppermute | solution.py:301
  131.0 11.3 %collective-permute-start = (bf16[64,96,256]{2,1,0:T(8,128)(2,1)S(1)}, bf16[64,96,256]{2,1,0:T(8,128)(2,1)}, u32[]{:S(2)}, u32[]{:S(2)}) collective-permute-start(bf16[64,96,256]{2,1,0:T(8,128)(2,1)S(1)} %all-to-all-done.own1), channel_id=1, source_target_pairs={{0,1},{1,0},{2,3},{3,2},{4,5},{5,4},{6,7},{7,6},{8,9},{9,8},{10,11... | collective-permute-start | bytes 9437192 | tf_op jit(solution)/shard_map/ppermute | solution.py:301
  131.0 34.6 %all-to-all-start.2 = ((bf16[64,32,512]{2,1,0:T(8,128)(2,1)}), bf16[64,32,512]{2,1,0:T(8,128)(2,1)}, u32[]{:S(2)}, u32[]{:S(2)}) async-start(bf16[64,32,512]{2,1,0:T(8,128)(2,1)} %get-tuple-element.23), calls=%async_computation.2 | async-start | bytes 4194304 | tf_op jit(solution)/shard_map/all_to_all | solution.py:298
  165.6 6.3 %collective-permute-start.2 = (bf16[64,32,512]{2,1,0:T(8,128)(2,1)}, bf16[64,32,512]{2,1,0:T(8,128)(2,1)S(1)}, u32[]{:S(2)}, u32[]{:S(2)}) collective-permute-start(bf16[64,32,512]{2,1,0:T(8,128)(2,1)} %all-to-all-done.2.own2), channel_id=1, source_target_pairs={{0,1},{1,0},{2,3},{3,2},{4,5},{5,4},{6,7},{7,6},{8,9},{9,8},{10,11... | collective-permute-start | bytes 6291464 | tf_op jit(solution)/shard_map/ppermute | solution.py:301
  171.9 1.3 copy-start.1
where the time goes:
time: 183 us
  Pallas kernels  73.7 us (40%)
  blocking collectives  60.4 us (33%)
  waiting for transfers between devices  24.5 us (13%)
  starting transfers between devices  22.6 us (12%)
    all_to_all x1, blocking collectives, exchange(): lax.all_to_all(value, 'wide', split_axis=0, concat_axis=0, tiled=True)  60.4 us
    pallas_call x2, Pallas kernels, spectra(): pl.pallas_call(functools.partial(spectra_kernel, first, count, split), ou...  46.1 us
    pallas_call x2, Pallas kernels, correlate(): pl.pallas_call(functools.partial(correlate_kernel, 1.0 / spectra_count, b...  27.6 us
    all_to_all x2, starting transfers between devices, exchange(): lax.all_to_all(value, 'wide', split_axis=0, concat_axis=0, tiled=True)  18 us
    all_to_all x2, waiting for transfers between devices, exchange(): lax.all_to_all(value, 'wide', split_axis=0, concat_axis=0, tiled=True)  15 us
    ppermute x3, waiting for transfers between devices, swap(): return lax.ppermute(value, 'narrow', [(0, 1), (1, 0)])  9.59 us
    ppermute x3, starting transfers between devices, swap(): return lax.ppermute(value, 'narrow', [(0, 1), (1, 0)])  4.65 us
  transfers between devices with their start and end apart: 5, of which 5 were waited for; matrix products, arithmetic and copies ran while one was open for 0% of the time, Pallas kernels for 26%

commit v1 on v0

--- a/solution.py
+++ b/solution.py
@@ -16,8 +16,10 @@
 LOCAL = 8
 PER = 6
 LANES = 128
-MADE = 15
+MADE = 8
+CORRELATE_BYTES = 26 * 2**20
 TOGETHER = 4
+PIECES = 1
 SPLIT = (4, 2)
 VMEM_BYTES = 60 * 2**20
 
@@ -193,12 +195,16 @@
         rows = pl.ds(16 * j, 16)
         copies = []
         for side, (first, second) in enumerate(((own1, own2), (other1, other2))):
-            copies.append(
-                pltpu.make_async_copy(first.at[:, head_rows, :], heads.at[j, side], in_sem.at[j, side, 0])
-            )
-            copies.append(
-                pltpu.make_async_copy(second.at[:, rows, :], tails.at[j, side], in_sem.at[j, side, 1])
-            )
+            for piece in range(PIECES):
+                some = pl.ds(piece * (WIDE // PIECES), WIDE // PIECES)
+                for which, (source, there, held) in enumerate(
+                    ((first, head_rows, heads), (second, rows, tails))
+                ):
+                    copies.append(
+                        pltpu.make_async_copy(
+                            source.at[some, there, :], held.at[j, side, some], in_sem.at[j, side, which, piece]
+                        )
+                    )
         return copies
 
     def outgoing(j, t):
@@ -274,11 +280,11 @@
             pltpu.VMEM((channels, 2, WIDE, 16, tail), jnp.bfloat16),
             pltpu.VMEM((2, 4, 512, spectra_count), jnp.bfloat16),
             pltpu.VMEM((MADE, 1024, LANES), jnp.float32),
-            pltpu.SemaphoreType.DMA((channels, 2, 2)),
+            pltpu.SemaphoreType.DMA((channels, 2, 2, PIECES)),
             pltpu.SemaphoreType.DMA((MADE,)),
         ],
         input_output_aliases=aliases,
-        compiler_params=pltpu.CompilerParams(vmem_limit_bytes=VMEM_BYTES),
+        compiler_params=pltpu.CompilerParams(vmem_limit_bytes=CORRELATE_BYTES),
         cost_estimate=pl.CostEstimate(
             flops=5 * channels * 8 * 256 * 256 * spectra_count, bytes_accessed=20 * 2**20, transcendentals=0
         ),

time: 183 us -> 182 us (level)
  Pallas kernels: 73.7 us -> 76.4 us
  waiting for transfers between devices: 24.5 us -> 21.8 us
    all_to_all x2, waiting for transfers between devices: 15 us -> 12.2 us  [exchange(): lax.all_to_all(value, 'wide', split_axis=0, concat_axis=0, tiled=True)]
    pallas_call x2, Pallas kernels: 27.6 us -> 30.2 us  [correlate(): pl.pallas_call(functools.partial(correlate_kernel, 1.0 / spectra_count, b...]
  transfers between devices with their start and end apart: 5 -> 5, of which waited for: 5 -> 5; matrix products, arithmetic and copies ran while one was open for 0% -> 0% of each run, Pallas kernels for 26% -> 28%
where the time goes in v1:
time: 182 us; the launch traced here: 181 us
  Pallas kernels  76.4 us (42%)
  blocking collectives  60.4 us (33%)
  starting transfers between devices  22.6 us (12%)
  waiting for transfers between devices  21.8 us (12%)
    all_to_all x1, blocking collectives, exchange(): lax.all_to_all(value, 'wide', split_axis=0, concat_axis=0, tiled=True)  60.4 us
    pallas_call x2, Pallas kernels, spectra(): pl.pallas_call(functools.partial(spectra_kernel, first, count, split), ou...  46.2 us
    pallas_call x2, Pallas kernels, correlate(): pl.pallas_call(functools.partial(correlate_kernel, 1.0 / spectra_count, b...  30.2 us
    all_to_all x2, starting transfers between devices, exchange(): lax.all_to_all(value, 'wide', split_axis=0, concat_axis=0, tiled=True)  18 us
    all_to_all x2, waiting for transfers between devices, exchange(): lax.all_to_all(value, 'wide', split_axis=0, concat_axis=0, tiled=True)  12.2 us
    ppermute x3, waiting for transfers between devices, swap(): return lax.ppermute(value, 'narrow', [(0, 1), (1, 0)])  9.59 us
    ppermute x3, starting transfers between devices, swap(): return lax.ppermute(value, 'narrow', [(0, 1), (1, 0)])  4.65 us
  transfers between devices with their start and end apart: 5, of which 5 were waited for; matrix products, arithmetic and copies ran while one was open for 0% of the time, Pallas kernels for 28%

profile of v1, /device:TPU:1, one launch (start us, length us, event | category | flops | bytes accessed | tf_op | source)
XLA Modules:
  0.0 181.5 jit_solution(5301424347596360939)
XLA Ops:
  0.0 16.8 %spectra.2 = bf16[64,96,256]{2,1,0:T(8,128)(2,1)} custom-call(s32[512]{0:T(512)} %flags_ref.3, bf16[8,2,2,192,779]{4,3,2,1,0:T(8,128)(2,1)} %bitcast.9, f32[12,8,384]{2,1,0:T(8,128)} %constant.4.clone.taps_ref, bf16[384,1152]{1,0:T(8,128)(2,1)} %constant.5.clone.table_ref), custom_call_target="tpu_custom_call" | custom-call | flops 3623878656 | bytes 6291456 | tf_op jit(solution)/shard_map/spectra/pallas_call | solution.py:163
  16.8 12.0 %all-to-all-start = ((bf16[64,96,256]{2,1,0:T(8,128)(2,1)}), bf16[64,96,256]{2,1,0:T(8,128)(2,1)S(1)}, u32[]{:S(2)}, u32[]{:S(2)}) async-start(bf16[64,96,256]{2,1,0:T(8,128)(2,1)} %spectra.2), calls=%async_computation | async-start | bytes 6291456 | tf_op jit(solution)/shard_map/all_to_all | solution.py:304
  28.8 29.3 %spectra.3 = (bf16[64,64,512]{2,1,0:T(8,128)(2,1)}, bf16[64,32,512]{2,1,0:T(8,128)(2,1)}) custom-call(s32[512]{0:T(512)} %flags_ref.3, bf16[8,2,2,192,779]{4,3,2,1,0:T(8,128)(2,1)} %bitcast.10, f32[12,8,384]{2,1,0:T(8,128)} %constant.4.clone.taps_ref, bf16[384,1152]{1,0:T(8,128)(2,1)} %constant.5.clone.table_ref), custom_call_target="tpu_custom_call" | custom-call | flops 7247757312 | bytes 12582912 | tf_op jit(solution)/shard_map/spectra/pallas_call | solution.py:163
  58.2 10.1 %all-to-all-done.own1 = bf16[64,96,256]{2,1,0:T(8,128)(2,1)S(1)} async-done(((bf16[64,96,256]{2,1,0:T(8,128)(2,1)}), bf16[64,96,256]{2,1,0:T(8,128)(2,1)S(1)}, u32[]{:S(2)}, u32[]{:S(2)}) %all-to-all-start) | async-done | bytes 3145760 | tf_op jit(solution)/shard_map/all_to_all | solution.py:304
  68.2 60.4 %all_to_all.15.own2 = bf16[64,64,512]{2,1,0:T(8,128)(2,1)} all-to-all(bf16[64,64,512]{2,1,0:T(8,128)(2,1)} %get-tuple-element.21), channel_id=1, replica_groups=mesh['wide'=64,'narrow'=2] {'wide'}, dimensions={0} | all-to-all | bytes 8388608 | tf_op jit(solution)/shard_map/all_to_all | solution.py:304
  128.6 0.0 copy-start
  128.6 2.3 %collective-permute-start.1 = (bf16[64,64,512]{2,1,0:T(8,128)(2,1)}, bf16[64,64,512]{2,1,0:T(8,128)(2,1)}, u32[]{:S(2)}, u32[]{:S(2)}) collective-permute-start(bf16[64,64,512]{2,1,0:T(8,128)(2,1)} %all_to_all.15.own2), channel_id=1, source_target_pairs={{0,1},{1,0},{2,3},{3,2},{4,5},{5,4},{6,7},{7,6},{8,9},{9,8},{10,11... | collective-permute-start | bytes 12582920 | tf_op jit(solution)/shard_map/ppermute | solution.py:307
  131.0 0.0 collective-permute-start
  131.0 6.0 %all-to-all-start.2 = ((bf16[64,32,512]{2,1,0:T(8,128)(2,1)}), bf16[64,32,512]{2,1,0:T(8,128)(2,1)}, u32[]{:S(2)}, u32[]{:S(2)}) async-start(bf16[64,32,512]{2,1,0:T(8,128)(2,1)} %get-tuple-element.23), calls=%async_computation.2 | async-start | bytes 4194304 | tf_op jit(solution)/shard_map/all_to_all | solution.py:304
  137.0 5.3 %collective-permute-done.other1 = bf16[64,96,256]{2,1,0:T(8,128)(2,1)} collective-permute-done((bf16[64,96,256]{2,1,0:T(8,128)(2,1)S(1)}, bf16[64,96,256]{2,1,0:T(8,128)(2,1)}, u32[]{:S(2)}, u32[]{:S(2)}) %collective-permute-start) | collective-permute-done | bytes 3145760 | tf_op jit(solution)/shard_map/ppermute | solution.py:307
  142.3 0.3 collective-permute-done.1.other2
  142.6 0.0 copy-done
  142.6 20.8 %correlate.2.rest_0_ = f32[5,6,1024,128]{3,2,1,0:T(8,128)} custom-call(s32[2,5]{1,0:T(2,128)S(1)} %bitcast.7, bf16[64,96,256]{2,1,0:T(8,128)(2,1)S(1)} %all-to-all-done.own1, bf16[64,64,512]{2,1,0:T(8,128)(2,1)} %all_to_all.15.own2, bf16[64,96,256]{2,1,0:T(8,128)(2,1)} %collective-permute-done.other1, bf16[64,64,512]{2,1,0:T(8,128)(2,1)} %collective-permute-done.1.other2), custom_call_target="tpu_custom_call" | custom-call | flops 8053063680 | bytes 20971520 | tf_op jit(solution)/shard_map/correlate/pallas_call | solution.py:273
  163.4 2.1 %all-to-all-done.2.own2 = bf16[64,32,512]{2,1,0:T(8,128)(2,1)} async-done(((bf16[64,32,512]{2,1,0:T(8,128)(2,1)}), bf16[64,32,512]{2,1,0:T(8,128)(2,1)}, u32[]{:S(2)}, u32[]{:S(2)}) %all-to-all-start.2) | async-done | bytes 2097184 | tf_op jit(solution)/shard_map/all_to_all | solution.py:304
  165.6 2.3 %collective-permute-start.2 = (bf16[64,32,512]{2,1,0:T(8,128)(2,1)}, bf16[64,32,512]{2,1,0:T(8,128)(2,1)S(1)}, u32[]{:S(2)}, u32[]{:S(2)}) collective-permute-start(bf16[64,32,512]{2,1,0:T(8,128)(2,1)} %all-to-all-done.2.own2), channel_id=1, source_target_pairs={{0,1},{1,0},{2,3},{3,2},{4,5},{5,4},{6,7},{7,6},{8,9},{9,8},{10,11... | collective-permute-start | bytes 6291464 | tf_op jit(solution)/shard_map/ppermute | solution.py:307
  167.9 4.0 %collective-permute-done.2.other2 = bf16[64,32,512]{2,1,0:T(8,128)(2,1)S(1)} collective-permute-done((bf16[64,32,512]{2,1,0:T(8,128)(2,1)}, bf16[64,32,512]{2,1,0:T(8,128)(2,1)S(1)}, u32[]{:S(2)}, u32[]{:S(2)}) %collective-permute-start.2) | collective-permute-done | bytes 2097184 | tf_op jit(solution)/shard_map/ppermute | solution.py:307
  171.9 9.4 %correlate.3 = f32[5,6,1024,128]{3,2,1,0:T(8,128)} custom-call(s32[2,5]{1,0:T(2,128)S(1)} %bitcast.8, bf16[64,96,256]{2,1,0:T(8,128)(2,1)S(1)} %all-to-all-done.own1, bf16[64,32,512]{2,1,0:T(8,128)(2,1)} %all-to-all-done.2.own2, bf16[64,96,256]{2,1,0:T(8,128)(2,1)} %collective-permute-done.other1, ...), custom_call_target="tpu_custom_call", output_to_operand_aliasing={{}: (5, {})} | custom-call | flops 4026531840 | bytes 20971520 | tf_op jit(solution)/shard_map/correlate/pallas_call | solution.py:273
Async XLA Ops:
  16.8 51.4 %all-to-all-start = ((bf16[64,96,256]{2,1,0:T(8,128)(2,1)}), bf16[64,96,256]{2,1,0:T(8,128)(2,1)S(1)}, u32[]{:S(2)}, u32[]{:S(2)}) async-start(bf16[64,96,256]{2,1,0:T(8,128)(2,1)} %spectra.2), calls=%async_computation | async-start | bytes 6291456 | tf_op jit(solution)/shard_map/all_to_all | solution.py:304
  128.6 14.0 %copy-start = (s32[5,2]{0,1:T(2,128)S(1)}, s32[5,2]{0,1:T(2,128)}, u32[]{:S(2)}) copy-start(s32[5,2]{0,1:T(2,128)} %param.7) | copy-start | bytes 124
  128.6 14.0 %collective-permute-start.1 = (bf16[64,64,512]{2,1,0:T(8,128)(2,1)}, bf16[64,64,512]{2,1,0:T(8,128)(2,1)}, u32[]{:S(2)}, u32[]{:S(2)}) collective-permute-start(bf16[64,64,512]{2,1,0:T(8,128)(2,1)} %all_to_all.15.own2), channel_id=1, source_target_pairs={{0,1},{1,0},{2,3},{3,2},{4,5},{5,4},{6,7},{7,6},{8,9},{9,8},{10,11... | collective-permute-start | bytes 12582920 | tf_op jit(solution)/shard_map/ppermute | solution.py:307
  131.0 11.3 %collective-permute-start = (bf16[64,96,256]{2,1,0:T(8,128)(2,1)S(1)}, bf16[64,96,256]{2,1,0:T(8,128)(2,1)}, u32[]{:S(2)}, u32[]{:S(2)}) collective-permute-start(bf16[64,96,256]{2,1,0:T(8,128)(2,1)S(1)} %all-to-all-done.own1), channel_id=1, source_target_pairs={{0,1},{1,0},{2,3},{3,2},{4,5},{5,4},{6,7},{7,6},{8,9},{9,8},{10,11... | collective-permute-start | bytes 9437192 | tf_op jit(solution)/shard_map/ppermute | solution.py:307
  131.0 34.6 %all-to-all-start.2 = ((bf16[64,32,512]{2,1,0:T(8,128)(2,1)}), bf16[64,32,512]{2,1,0:T(8,128)(2,1)}, u32[]{:S(2)}, u32[]{:S(2)}) async-start(bf16[64,32,512]{2,1,0:T(8,128)(2,1)} %get-tuple-element.23), calls=%async_computation.2 | async-start | bytes 4194304 | tf_op jit(solution)/shard_map/all_to_all | solution.py:304
  165.6 6.3 %collective-permute-start.2 = (bf16[64,32,512]{2,1,0:T(8,128)(2,1)}, bf16[64,32,512]{2,1,0:T(8,128)(2,1)S(1)}, u32[]{:S(2)}, u32[]{:S(2)}) collective-permute-start(bf16[64,32,512]{2,1,0:T(8,128)(2,1)} %all-to-all-done.2.own2), channel_id=1, source_target_pairs={{0,1},{1,0},{2,3},{3,2},{4,5},{5,4},{6,7},{7,6},{8,9},{9,8},{10,11... | collective-permute-start | bytes 6291464 | tf_op jit(solution)/shard_map/ppermute | solution.py:307

commit v2 on v1

--- a/solution.py
+++ b/solution.py
@@ -106,9 +106,9 @@
                     at = third * 2 * F + column * LANES
                     framed[start : start + 64, at : at + LANES] = half
         product = lax.dot_general(
-            table_ref[...], framed[...], (((1,), (1,)), ((), ())), preferred_element_type=jnp.float32
+            framed[...], table_ref[...], (((1,), (1,)), ((), ())), preferred_element_type=jnp.float32
         )
-        product = product * keep
+        product = product.T * keep
         for tile in range(count // LANES):
             turned[tile, pl.ds(i, 2 * F, stride=LOCAL), :] = product[
                 :, tile * LANES : (tile + 1) * LANES
@@ -217,13 +217,13 @@
         copy.start()
     dims = (((1,), (1,)), ((), ()))
     for j in range(channels):
-        for copy in incoming(j):
-            copy.wait()
-        if j + 1 < channels:
-            for copy in incoming(j + 1):
-                copy.start()
         hold = j % 2
         for side in range(2):
+            for copy in incoming(j)[2 * side * PIECES : 2 * (side + 1) * PIECES]:
+                copy.wait()
+            if side == 0 and j + 1 < channels:
+                for copy in incoming(j + 1):
+                    copy.start()
             half = mine if side == 0 else 1 - mine
             for part in range(2):
                 sources = slice(part * 32, part * 32 + 32)

time: 182 us -> 182 us (level)
  no operation moved by 1% of the time
where the time goes in v2:
time: 182 us; the launch traced here: 181 us
  Pallas kernels  76.6 us (42%)
  blocking collectives  60.4 us (33%)
  starting transfers between devices  22.8 us (13%)
  waiting for transfers between devices  21.2 us (12%)
    all_to_all x1, blocking collectives, exchange(): lax.all_to_all(value, 'wide', split_axis=0, concat_axis=0, tiled=True)  60.4 us
    pallas_call x2, Pallas kernels, spectra(): pl.pallas_call(functools.partial(spectra_kernel, first, count, split), ou...  46.6 us
    pallas_call x2, Pallas kernels, correlate(): pl.pallas_call(functools.partial(correlate_kernel, 1.0 / spectra_count, b...  29.9 us
    all_to_all x2, starting transfers between devices, exchange(): lax.all_to_all(value, 'wide', split_axis=0, concat_axis=0, tiled=True)  18.2 us
    all_to_all x2, waiting for transfers between devices, exchange(): lax.all_to_all(value, 'wide', split_axis=0, concat_axis=0, tiled=True)  11.8 us
    ppermute x3, waiting for transfers between devices, swap(): return lax.ppermute(value, 'narrow', [(0, 1), (1, 0)])  9.41 us
    ppermute x3, starting transfers between devices, swap(): return lax.ppermute(value, 'narrow', [(0, 1), (1, 0)])  4.65 us
  transfers between devices with their start and end apart: 5, of which 5 were waited for; matrix products, arithmetic and copies ran while one was open for 0% of the time, Pallas kernels for 28%

profile of v2, /device:TPU:1, one launch (start us, length us, event | category | flops | bytes accessed | tf_op | source)
XLA Modules:
  0.0 181.2 jit_solution(8274327018853451565)
XLA Ops:
  0.0 16.6 %spectra.2 = bf16[64,96,256]{2,1,0:T(8,128)(2,1)} custom-call(s32[512]{0:T(512)} %flags_ref.3, bf16[8,2,2,192,779]{4,3,2,1,0:T(8,128)(2,1)} %bitcast.9, f32[12,8,384]{2,1,0:T(8,128)} %constant.4.clone.taps_ref, bf16[384,1152]{1,0:T(8,128)(2,1)} %constant.5.clone.table_ref), custom_call_target="tpu_custom_call" | custom-call | flops 3623878656 | bytes 6291456 | tf_op jit(solution)/shard_map/spectra/pallas_call | solution.py:163
  16.6 12.0 %all-to-all-start = ((bf16[64,96,256]{2,1,0:T(8,128)(2,1)}), bf16[64,96,256]{2,1,0:T(8,128)(2,1)S(1)}, u32[]{:S(2)}, u32[]{:S(2)}) async-start(bf16[64,96,256]{2,1,0:T(8,128)(2,1)} %spectra.2), calls=%async_computation | async-start | bytes 6291456 | tf_op jit(solution)/shard_map/all_to_all | solution.py:304
  28.6 30.1 %spectra.3 = (bf16[64,64,512]{2,1,0:T(8,128)(2,1)}, bf16[64,32,512]{2,1,0:T(8,128)(2,1)}) custom-call(s32[512]{0:T(512)} %flags_ref.3, bf16[8,2,2,192,779]{4,3,2,1,0:T(8,128)(2,1)} %bitcast.10, f32[12,8,384]{2,1,0:T(8,128)} %constant.4.clone.taps_ref, bf16[384,1152]{1,0:T(8,128)(2,1)} %constant.5.clone.table_ref), custom_call_target="tpu_custom_call" | custom-call | flops 7247757312 | bytes 12582912 | tf_op jit(solution)/shard_map/spectra/pallas_call | solution.py:163
  58.6 9.3 %all-to-all-done.own1 = bf16[64,96,256]{2,1,0:T(8,128)(2,1)S(1)} async-done(((bf16[64,96,256]{2,1,0:T(8,128)(2,1)}), bf16[64,96,256]{2,1,0:T(8,128)(2,1)S(1)}, u32[]{:S(2)}, u32[]{:S(2)}) %all-to-all-start) | async-done | bytes 3145760 | tf_op jit(solution)/shard_map/all_to_all | solution.py:304
  68.0 60.4 %all_to_all.15.own2 = bf16[64,64,512]{2,1,0:T(8,128)(2,1)} all-to-all(bf16[64,64,512]{2,1,0:T(8,128)(2,1)} %get-tuple-element.21), channel_id=1, replica_groups=mesh['wide'=64,'narrow'=2] {'wide'}, dimensions={0} | all-to-all | bytes 8388608 | tf_op jit(solution)/shard_map/all_to_all | solution.py:304
  128.4 0.0 copy-start
  128.4 2.3 %collective-permute-start.1 = (bf16[64,64,512]{2,1,0:T(8,128)(2,1)}, bf16[64,64,512]{2,1,0:T(8,128)(2,1)}, u32[]{:S(2)}, u32[]{:S(2)}) collective-permute-start(bf16[64,64,512]{2,1,0:T(8,128)(2,1)} %all_to_all.15.own2), channel_id=1, source_target_pairs={{0,1},{1,0},{2,3},{3,2},{4,5},{5,4},{6,7},{7,6},{8,9},{9,8},{10,11... | collective-permute-start | bytes 12582920 | tf_op jit(solution)/shard_map/ppermute | solution.py:307
  130.7 0.0 collective-permute-start
  130.7 6.2 %all-to-all-start.2 = ((bf16[64,32,512]{2,1,0:T(8,128)(2,1)}), bf16[64,32,512]{2,1,0:T(8,128)(2,1)}, u32[]{:S(2)}, u32[]{:S(2)}) async-start(bf16[64,32,512]{2,1,0:T(8,128)(2,1)} %get-tuple-element.23), calls=%async_computation.2 | async-start | bytes 4194304 | tf_op jit(solution)/shard_map/all_to_all | solution.py:304
  136.9 5.1 %collective-permute-done.other1 = bf16[64,96,256]{2,1,0:T(8,128)(2,1)} collective-permute-done((bf16[64,96,256]{2,1,0:T(8,128)(2,1)S(1)}, bf16[64,96,256]{2,1,0:T(8,128)(2,1)}, u32[]{:S(2)}, u32[]{:S(2)}) %collective-permute-start) | collective-permute-done | bytes 3145760 | tf_op jit(solution)/shard_map/ppermute | solution.py:307
  142.0 0.3 collective-permute-done.1.other2
  142.4 0.0 copy-done
  142.4 20.6 %correlate.2.rest_0_ = f32[5,6,1024,128]{3,2,1,0:T(8,128)} custom-call(s32[2,5]{1,0:T(2,128)S(1)} %bitcast.7, bf16[64,96,256]{2,1,0:T(8,128)(2,1)S(1)} %all-to-all-done.own1, bf16[64,64,512]{2,1,0:T(8,128)(2,1)} %all_to_all.15.own2, bf16[64,96,256]{2,1,0:T(8,128)(2,1)} %collective-permute-done.other1, bf16[64,64,512]{2,1,0:T(8,128)(2,1)} %collective-permute-done.1.other2), custom_call_target="tpu_custom_call" | custom-call | flops 8053063680 | bytes 20971520 | tf_op jit(solution)/shard_map/correlate/pallas_call | solution.py:273
  163.0 2.5 %all-to-all-done.2.own2 = bf16[64,32,512]{2,1,0:T(8,128)(2,1)} async-done(((bf16[64,32,512]{2,1,0:T(8,128)(2,1)}), bf16[64,32,512]{2,1,0:T(8,128)(2,1)}, u32[]{:S(2)}, u32[]{:S(2)}) %all-to-all-start.2) | async-done | bytes 2097184 | tf_op jit(solution)/shard_map/all_to_all | solution.py:304
  165.5 2.3 %collective-permute-start.2 = (bf16[64,32,512]{2,1,0:T(8,128)(2,1)}, bf16[64,32,512]{2,1,0:T(8,128)(2,1)S(1)}, u32[]{:S(2)}, u32[]{:S(2)}) collective-permute-start(bf16[64,32,512]{2,1,0:T(8,128)(2,1)} %all-to-all-done.2.own2), channel_id=1, source_target_pairs={{0,1},{1,0},{2,3},{3,2},{4,5},{5,4},{6,7},{7,6},{8,9},{9,8},{10,11... | collective-permute-start | bytes 6291464 | tf_op jit(solution)/shard_map/ppermute | solution.py:307
  167.8 4.0 %collective-permute-done.2.other2 = bf16[64,32,512]{2,1,0:T(8,128)(2,1)S(1)} collective-permute-done((bf16[64,32,512]{2,1,0:T(8,128)(2,1)}, bf16[64,32,512]{2,1,0:T(8,128)(2,1)S(1)}, u32[]{:S(2)}, u32[]{:S(2)}) %collective-permute-start.2) | collective-permute-done | bytes 2097184 | tf_op jit(solution)/shard_map/ppermute | solution.py:307
  171.8 9.3 %correlate.3 = f32[5,6,1024,128]{3,2,1,0:T(8,128)} custom-call(s32[2,5]{1,0:T(2,128)S(1)} %bitcast.8, bf16[64,96,256]{2,1,0:T(8,128)(2,1)S(1)} %all-to-all-done.own1, bf16[64,32,512]{2,1,0:T(8,128)(2,1)} %all-to-all-done.2.own2, bf16[64,96,256]{2,1,0:T(8,128)(2,1)} %collective-permute-done.other1, ...), custom_call_target="tpu_custom_call", output_to_operand_aliasing={{}: (5, {})} | custom-call | flops 4026531840 | bytes 20971520 | tf_op jit(solution)/shard_map/correlate/pallas_call | solution.py:273
Async XLA Ops:
  16.6 51.4 %all-to-all-start = ((bf16[64,96,256]{2,1,0:T(8,128)(2,1)}), bf16[64,96,256]{2,1,0:T(8,128)(2,1)S(1)}, u32[]{:S(2)}, u32[]{:S(2)}) async-start(bf16[64,96,256]{2,1,0:T(8,128)(2,1)} %spectra.2), calls=%async_computation | async-start | bytes 6291456 | tf_op jit(solution)/shard_map/all_to_all | solution.py:304
  128.4 14.0 %copy-start = (s32[5,2]{0,1:T(2,128)S(1)}, s32[5,2]{0,1:T(2,128)}, u32[]{:S(2)}) copy-start(s32[5,2]{0,1:T(2,128)} %param.7) | copy-start | bytes 124
  128.4 14.0 %collective-permute-start.1 = (bf16[64,64,512]{2,1,0:T(8,128)(2,1)}, bf16[64,64,512]{2,1,0:T(8,128)(2,1)}, u32[]{:S(2)}, u32[]{:S(2)}) collective-permute-start(bf16[64,64,512]{2,1,0:T(8,128)(2,1)} %all_to_all.15.own2), channel_id=1, source_target_pairs={{0,1},{1,0},{2,3},{3,2},{4,5},{5,4},{6,7},{7,6},{8,9},{9,8},{10,11... | collective-permute-start | bytes 12582920 | tf_op jit(solution)/shard_map/ppermute | solution.py:307
  130.7 11.3 %collective-permute-start = (bf16[64,96,256]{2,1,0:T(8,128)(2,1)S(1)}, bf16[64,96,256]{2,1,0:T(8,128)(2,1)}, u32[]{:S(2)}, u32[]{:S(2)}) collective-permute-start(bf16[64,96,256]{2,1,0:T(8,128)(2,1)S(1)} %all-to-all-done.own1), channel_id=1, source_target_pairs={{0,1},{1,0},{2,3},{3,2},{4,5},{5,4},{6,7},{7,6},{8,9},{9,8},{10,11... | collective-permute-start | bytes 9437192 | tf_op jit(solution)/shard_map/ppermute | solution.py:307
  130.7 34.7 %all-to-all-start.2 = ((bf16[64,32,512]{2,1,0:T(8,128)(2,1)}), bf16[64,32,512]{2,1,0:T(8,128)(2,1)}, u32[]{:S(2)}, u32[]{:S(2)}) async-start(bf16[64,32,512]{2,1,0:T(8,128)(2,1)} %get-tuple-element.23), calls=%async_computation.2 | async-start | bytes 4194304 | tf_op jit(solution)/shard_map/all_to_all | solution.py:304
  165.5 6.3 %collective-permute-start.2 = (bf16[64,32,512]{2,1,0:T(8,128)(2,1)}, bf16[64,32,512]{2,1,0:T(8,128)(2,1)S(1)}, u32[]{:S(2)}, u32[]{:S(2)}) collective-permute-start(bf16[64,32,512]{2,1,0:T(8,128)(2,1)} %all-to-all-done.2.own2), channel_id=1, source_target_pairs={{0,1},{1,0},{2,3},{3,2},{4,5},{5,4},{6,7},{7,6},{8,9},{9,8},{10,11... | collective-permute-start | bytes 6291464 | tf_op jit(solution)/shard_map/ppermute | solution.py:307
